TPU v7x, 32 devices: a whole 2x2x4 slice. The times are simulated.
32 devices in a mesh: dp: 4 (over z), ctx: 8 (over y, x, core).
Axes of the slice: x: 2, y: 2, z: 4, core: 2. Of those that a mesh axis runs over, the one named last changes fastest.
Arguments:
- inputs: bfloat16 [4, 2048, 2048], P('dp', 'ctx'), may hold values from -6 to 6
- places: int32 [4, 2048], P('dp', 'ctx'), may hold values from 0 to 2047, as said below
- cotangent: bfloat16 [4, 2048, 2048], P('dp', 'ctx'), may hold values from -6 to 6
- attn_gain: float32 [2048], replicated, may hold values from 0.5 to 1.5
- w_qkv: bfloat16 [2048, 1536], P(('dp', 'ctx')), may hold values from -0.125 to 0.125
- q_gain: float32 [64], replicated, may hold values from 0.1 to 1.9
- k_gain: float32 [64], replicated, may hold values from 0.1 to 1.9
- w_out: bfloat16 [1024, 2048], P(('dp', 'ctx')), may hold values from -6 to 6
- ffn_gain: float32 [2048], replicated, may hold values from 0.5 to 1.5
- w_gateup: bfloat16 [2048, 2048], P(('dp', 'ctx')), may hold values from -0.125 to 0.125
- w_down: bfloat16 [1024, 2048], P(('dp', 'ctx')), may hold values from -0.1875 to 0.1875
Outputs:
- layer_output: bfloat16 [4, 2048, 2048], P('dp', 'ctx')
- grad_inputs: bfloat16 [4, 2048, 2048], P('dp', 'ctx')
- grad_attn_gain: float32 [2048], replicated
- grad_w_qkv: float32 [2048, 1536], P(('dp', 'ctx'))
- grad_q_gain: float32 [64], replicated
- grad_k_gain: float32 [64], replicated
- grad_w_out: float32 [1024, 2048], P(('dp', 'ctx'))
- grad_ffn_gain: float32 [2048], replicated
- grad_w_gateup: float32 [2048, 2048], P(('dp', 'ctx'))
- grad_w_down: float32 [1024, 2048], P(('dp', 'ctx'))
Inputs may be any that keep to these rules, and one draw needn't show every extreme that they name: Each row of places holds every position 0 to 2047 once. Cut a sequence into 16 blocks of 128 consecutive positions; each aligned block of 256 entries (one device's tokens) is a block b in increasing order followed by block 15 - b in increasing order.
All inputs are finite; a program needn't handle non-finite values.
Results may differ from a plain program's by a relative error of at most 0.02.
Values may be sent and summed in bfloat16 or wider, within the bound.
A program may use at most 128 MiB of HBM per device.

v0:
```python
import math

import jax
import jax.numpy as jnp
from jax import lax
from jax.sharding import PartitionSpec as P

HEADS = 16
GROUPS = 4
HEAD_DIM = 64
FF = 1024


epsilon = 1e-06


def norm_rows(values, gain_vec):
    return (
        values * lax.rsqrt(jnp.mean(values * values, axis=-1, keepdims=True) + epsilon) * gain_vec
    )


def rotate(values, positions):
    half_dim = values.shape[-1] // 2
    frequency = jnp.exp(
        jnp.arange(half_dim).astype(jnp.float32) * (-2.0 * math.log(10000.0) / values.shape[-1])
    )
    angles = positions.astype(jnp.float32)[:, None] * frequency[None, :]
    cosine = jnp.cos(angles)[:, None, :]
    sine = jnp.sin(angles)[:, None, :]
    first = values[..., :half_dim]
    second = values[..., half_dim:]
    return jnp.concatenate(
        [first * cosine - second * sine, second * cosine + first * sine], axis=-1
    )


def project_heads(qkv_all, positions, q_gain, k_gain):
    tok_rows = qkv_all.shape[0]
    q_cols = HEADS * HEAD_DIM
    k_cols = GROUPS * HEAD_DIM
    queries = qkv_all[:, :q_cols].reshape(tok_rows, HEADS, HEAD_DIM)
    keys_raw = qkv_all[:, q_cols : q_cols + k_cols].reshape(tok_rows, GROUPS, HEAD_DIM)
    values = qkv_all[:, q_cols + k_cols :].reshape(tok_rows, GROUPS, HEAD_DIM)
    return (
        rotate(norm_rows(queries, q_gain), positions),
        rotate(norm_rows(keys_raw, k_gain), positions),
        values,
    )


def gated(gate_up):
    return jax.nn.silu(gate_up[:, :FF]) * gate_up[:, FF:]


def per_device(
    inputs, places, cotangent, attn_gain, w_qkv, q_gain, k_gain, w_out, ffn_gain, w_gateup, w_down
):
    tok_rows = inputs.shape[1]
    repeat = HEADS // GROUPS
    score_scale = HEAD_DIM ** (-0.5)
    here_f = inputs[0].astype(jnp.float32)
    own_places = places[0]
    qkv_w, out_w = (
        lax.all_gather(w_qkv, ("dp", "ctx"), axis=0, tiled=True),
        lax.all_gather(w_out, ("dp", "ctx"), axis=0, tiled=True),
    )
    h_attn_f, pull_attn = jax.vjp(norm_rows, here_f, attn_gain)
    h_attn = h_attn_f.astype(jnp.bfloat16)
    qkv_all = jnp.dot(h_attn, qkv_w, preferred_element_type=jnp.float32)

    def heads_of(qkv_in, gain_q, gain_k):
        return project_heads(qkv_in, own_places, gain_q, gain_k)

    (queries, keys_f, values), pull_heads = jax.vjp(heads_of, qkv_all, q_gain, k_gain)
    query_b = queries.astype(jnp.bfloat16).reshape(tok_rows, GROUPS, repeat, HEAD_DIM)
    key_b = keys_f.astype(jnp.bfloat16)
    value_b = values.astype(jnp.bfloat16)
    all_keys, all_values = (
        lax.all_gather(key_b, "ctx", axis=0, tiled=True),
        lax.all_gather(value_b, "ctx", axis=0, tiled=True),
    )
    all_places = lax.all_gather(own_places, "ctx", axis=0, tiled=True)
    blocks = lax.axis_size("ctx")
    key_blocks = all_keys.reshape(blocks, tok_rows, GROUPS, HEAD_DIM)
    value_blocks = all_values.reshape(blocks, tok_rows, GROUPS, HEAD_DIM)
    place_blocks = all_places.reshape(blocks, tok_rows)

    def score_block(key_blk, place_blk):
        scores = (
            jnp.einsum("igrd,jgd->grij", query_b, key_blk, preferred_element_type=jnp.float32)
            * score_scale
        )
        allowed = place_blk[None, :] <= own_places[:, None]
        return (scores, allowed)

    def max_step(state_pair, entries):
        row_top, row_total = state_pair
        scores, allowed = score_block(entries[0], entries[1])
        scores = jnp.where(allowed, scores, -1e30)
        new_top = jnp.maximum(row_top, jnp.max(scores, axis=-1))
        row_total = row_total * jnp.exp(row_top - new_top) + jnp.sum(
            jnp.where(allowed, jnp.exp(scores - new_top[..., None]), 0.0), axis=-1
        )
        return ((new_top, row_total), None)

    start_pair = (
        jnp.full((GROUPS, repeat, tok_rows), -1e30, jnp.float32),
        jnp.zeros((GROUPS, repeat, tok_rows), jnp.float32),
    )
    (row_top, row_total), _ = lax.scan(max_step, start_pair, (key_blocks, place_blocks))
    log_total = row_top + jnp.log(row_total)

    def out_step(accum, entries):
        scores, allowed = score_block(entries[0], entries[1])
        weights_b = jnp.where(allowed, jnp.exp(scores - log_total[..., None]), 0.0).astype(
            jnp.bfloat16
        )
        return (
            accum
            + jnp.einsum(
                "grij,jgd->igrd", weights_b, entries[2], preferred_element_type=jnp.float32
            ),
            None,
        )

    mixed_f, _ = lax.scan(
        out_step,
        jnp.zeros((tok_rows, GROUPS, repeat, HEAD_DIM), jnp.float32),
        (key_blocks, place_blocks, value_blocks),
    )
    mixed_b = mixed_f.reshape(tok_rows, HEADS * HEAD_DIM).astype(jnp.bfloat16)
    attn_out = jnp.dot(mixed_b, out_w, preferred_element_type=jnp.float32)
    residual = here_f + attn_out
    gateup_w, down_w = (
        lax.all_gather(w_gateup, ("dp", "ctx"), axis=0, tiled=True),
        lax.all_gather(w_down, ("dp", "ctx"), axis=0, tiled=True),
    )
    h_ffn_f, pull_ffn = jax.vjp(norm_rows, residual, ffn_gain)
    h_ffn = h_ffn_f.astype(jnp.bfloat16)
    gate_up = jnp.dot(h_ffn, gateup_w, preferred_element_type=jnp.float32)
    act_f, pull_gate = jax.vjp(gated, gate_up)
    act_b = act_f.astype(jnp.bfloat16)
    result = residual + jnp.dot(act_b, down_w, preferred_element_type=jnp.float32)
    layer_output = result.astype(jnp.bfloat16)[None]
    gateup_w, down_w = (
        lax.all_gather(w_gateup, ("dp", "ctx"), axis=0, tiled=True),
        lax.all_gather(w_down, ("dp", "ctx"), axis=0, tiled=True),
    )
    grad_out = cotangent[0]
    grad_act = jnp.dot(grad_out, down_w.T, preferred_element_type=jnp.float32)
    grad_down = jnp.dot(act_b.T, grad_out, preferred_element_type=jnp.float32)
    grad_gu_b = pull_gate(grad_act)[0].astype(jnp.bfloat16)
    grad_gateup = jnp.dot(h_ffn.T, grad_gu_b, preferred_element_type=jnp.float32)
    grad_h_ffn = jnp.dot(grad_gu_b, gateup_w.T, preferred_element_type=jnp.float32)
    grad_resid_part, grad_ffn_gain = pull_ffn(grad_h_ffn)
    grad_residual = grad_out.astype(jnp.float32) + grad_resid_part
    grad_gateup_own, grad_down_own = (
        lax.psum_scatter(grad_gateup, ("dp", "ctx"), scatter_dimension=0, tiled=True),
        lax.psum_scatter(grad_down, ("dp", "ctx"), scatter_dimension=0, tiled=True),
    )
    qkv_w, out_w = (
        lax.all_gather(w_qkv, ("dp", "ctx"), axis=0, tiled=True),
        lax.all_gather(w_out, ("dp", "ctx"), axis=0, tiled=True),
    )
    grad_attn_b = grad_residual.astype(jnp.bfloat16)
    grad_out_w = jnp.dot(mixed_b.T, grad_attn_b, preferred_element_type=jnp.float32)
    grad_mixed_b = (
        jnp.dot(grad_attn_b, out_w.T, preferred_element_type=jnp.float32)
        .astype(jnp.bfloat16)
        .reshape(tok_rows, GROUPS, repeat, HEAD_DIM)
    )
    row_delta = jnp.transpose(
        jnp.sum(grad_mixed_b.astype(jnp.float32) * mixed_f, axis=-1), (1, 2, 0)
    )

    def back_step(grad_query, entries):
        key_blk, place_blk, value_blk = entries
        scores, allowed = score_block(key_blk, place_blk)
        weights_f = jnp.where(allowed, jnp.exp(scores - log_total[..., None]), 0.0)
        weights_b = weights_f.astype(jnp.bfloat16)
        grad_value = jnp.einsum(
            "grij,igrd->jgd", weights_b, grad_mixed_b, preferred_element_type=jnp.float32
        )
        grad_prob = jnp.einsum(
            "igrd,jgd->grij", grad_mixed_b, value_blk, preferred_element_type=jnp.float32
        )
        grad_score = (weights_f * (grad_prob - row_delta[..., None])).astype(jnp.bfloat16)
        grad_query = grad_query + jnp.einsum(
            "grij,jgd->igrd", grad_score, key_blk, preferred_element_type=jnp.float32
        )
        grad_key = (
            jnp.einsum("grij,igrd->jgd", grad_score, query_b, preferred_element_type=jnp.float32)
            * score_scale
        )
        return (
            grad_query,
            jnp.concatenate(
                [
                    grad_key.reshape(tok_rows, GROUPS * HEAD_DIM),
                    grad_value.reshape(tok_rows, GROUPS * HEAD_DIM),
                ],
                axis=1,
            ),
        )

    grad_query, kv_terms = lax.scan(
        back_step,
        jnp.zeros((tok_rows, GROUPS, repeat, HEAD_DIM), jnp.float32),
        (key_blocks, place_blocks, value_blocks),
    )
    grad_query = grad_query * score_scale
    kv_own = lax.psum_scatter(
        kv_terms.reshape(blocks * tok_rows, 2 * GROUPS * HEAD_DIM).astype(jnp.bfloat16),
        "ctx",
        scatter_dimension=0,
        tiled=True,
    ).astype(jnp.float32)
    grad_key_own = kv_own[:, : GROUPS * HEAD_DIM].reshape(tok_rows, GROUPS, HEAD_DIM)
    grad_value_own = kv_own[:, GROUPS * HEAD_DIM :].reshape(tok_rows, GROUPS, HEAD_DIM)
    grad_qkv_f, grad_q_gain, grad_k_gain = pull_heads(
        (grad_query.reshape(tok_rows, HEADS, HEAD_DIM), grad_key_own, grad_value_own)
    )
    grad_qkv_b = grad_qkv_f.astype(jnp.bfloat16)
    grad_qkv_w = jnp.dot(h_attn.T, grad_qkv_b, preferred_element_type=jnp.float32)
    grad_h_attn = jnp.dot(grad_qkv_b, qkv_w.T, preferred_element_type=jnp.float32)
    grad_here_part, grad_attn_gain = pull_attn(grad_h_attn)
    grad_inputs = (grad_residual + grad_here_part).astype(jnp.bfloat16)[None]
    grad_qkv_own, grad_out_own = (
        lax.psum_scatter(grad_qkv_w, ("dp", "ctx"), scatter_dimension=0, tiled=True),
        lax.psum_scatter(grad_out_w, ("dp", "ctx"), scatter_dimension=0, tiled=True),
    )
    gain_attn, gain_query, gain_key, gain_ffn = lax.psum(
        (grad_attn_gain, grad_q_gain, grad_k_gain, grad_ffn_gain), ("dp", "ctx")
    )
    return (
        layer_output,
        grad_inputs,
        gain_attn,
        grad_qkv_own,
        gain_query,
        gain_key,
        grad_out_own,
        gain_ffn,
        grad_gateup_own,
        grad_down_own,
    )


def solution(mesh):
    in_specs = (
        P("dp", "ctx", None),
        P("dp", "ctx"),
        P("dp", "ctx", None),
        P(),
        P(("dp", "ctx"), None),
        P(),
        P(),
        P(("dp", "ctx"), None),
        P(),
        P(("dp", "ctx"), None),
        P(("dp", "ctx"), None),
    )
    out_specs = (
        P("dp", "ctx", None),
        P("dp", "ctx", None),
        P(),
        P(("dp", "ctx"), None),
        P(),
        P(),
        P(("dp", "ctx"), None),
        P(),
        P(("dp", "ctx"), None),
        P(("dp", "ctx"), None),
    )
    return jax.shard_map(
        per_device, mesh=mesh, in_specs=in_specs, out_specs=out_specs, check_vma=False
    )
```

profile of v0, /device:TPU:0, one launch (start us, length us, event | category | flops | bytes accessed | tf_op | source)
XLA Modules:
  0.0 1141.3 jit_solution(15101829259816148174)
XLA Ops:
  11.0 72.2 %all-gather.8.cloned.1.call-done = bf16[2048,1536]{1,0:T(8,128)(2,1)} async-done(((bf16[64,1536]{1,0:T(8,128)(2,1)}), bf16[2048,1536]{1,0:T(8,128)(2,1)}) %all-gather.8.cloned.1.call-update) | async-done | bytes 6291472 | tf_op jit(solution)/shard_map/all_gather | solution.py:65
  83.1 5.0 fusion.67
  92.0 8.9 all-gather
  106.7 4.9 all-gather.12.cloned.1.call-done
  113.9 56.0 %while.37 = (s32[]{:T(128)}, f32[4,4,256]{2,1,0:T(4,128)S(1)}, f32[4,4,256]{2,1,0:T(4,128)S(1)}, s32[8,256]{1,0:T(8,128)S(1)}, s32[1,256]{1,0:T(1,128)S(1)}, /*i...) while((s32[]{:T(128)}, f32[4,4,256]{2,1,0:T(4,128)S(1)}, ...), condition=%wide.region_6.7_spmd.clone, body=%wide.region_3.6_spmd.clone.sunk | while | flops 142692352 | bytes 9457784 | solution.py:111
  174.4 29.3 %while.38 = (s32[]{:T(128)}, f32[256,4,4,64]{0,3,2,1:T(8,128)S(1)}, bf16[8,256,4,64]{1,3,2,0:T(8,128)(2,1)}, s32[8,256]{1,0:T(8,128)S(1)}, s32[1,256]{1,0:T(1,12...) while((s32[]{:T(128)}, f32[256,4,4,64]{0,3,2,1:T(8,128)S(1)}, ...), condition=%wide.region_8.9_spmd.clone, body=%wide.region_7.8_spmd.clone.sunk | while | flops 273219584 | bytes 4083843 | solution.py:127
  206.0 3.9 multiply_reduce_fusion.2
  209.9 71.3 %all-gather.16.cloned.1.call-done = bf16[2048,2048]{1,0:T(8,128)(2,1)} async-done(((bf16[64,2048]{1,0:T(8,128)(2,1)}), bf16[2048,2048]{1,0:T(8,128)(2,1)}) %all-gather.16.cloned.1.call-update) | async-done | bytes 8388624 | tf_op jit(solution)/shard_map/all_gather | solution.py:136
  281.2 7.1 fusion.79
  288.2 56.3 %all-gather.18.cloned.1.call-done = bf16[1024,2048]{1,0:T(8,128)(2,1)} async-done(((bf16[32,2048]{1,0:T(8,128)(2,1)}), bf16[1024,2048]{1,0:T(8,128)(2,1)}) %all-gather.18.cloned.1.call-update) | async-done | bytes 4194320 | tf_op jit(solution)/shard_map/all_gather | solution.py:137
  344.5 5.7 fusion.71
  360.8 90.9 %while.39 = (s32[]{:T(128)}, f32[256,4,4,64]{0,3,2,1:T(8,128)}, bf16[8,256,512]{2,1,0:T(8,128)(2,1)}, bf16[8,256,4,64]{1,3,2,0:T(8,128)(2,1)}, s32[8,256]{1,0:T(...) while((s32[]{:T(128)}, f32[256,4,4,64]{0,3,2,1:T(8,128)}, ...), condition=%wide.region_13.14_spmd.clone, body=%wide.region_12.13_spmd.clone.sunk | while | flops 682819584 | bytes 59298096 | solution.py:207
  453.3 4.6 fusion.62
  459.2 5.5 fusion.57
  471.9 19.7 %reduce-scatter.6.cloned.1.call-done = bf16[256,512]{1,0:T(8,128)(2,1)} async-done(((bf16[2048,512]{1,0:T(8,128)(2,1)}), bf16[256,512]{1,0:T(8,128)(2,1)}) %reduce-scatter.6.cloned.1.call-update) | async-done | bytes 262160 | tf_op jit(solution)/shard_map/reduce_scatter | solution.py:213
  498.3 7.7 fusion.65
  506.8 10.4 fusion.69
  517.3 5.5 fusion.46
  522.8 6.2 fusion.48
  528.9 41.4 %all-reduce.9 = (f32[2048]{0:T(1024)}, f32[64]{0:T(128)}, f32[64]{0:T(128)}, f32[2048]{0:T(1024)}) all-reduce(f32[2048]{0:T(1024)S(1)} %get-tuple-element.287, f32[64]{0:T(128)S(1)} %copy-done.42, f32[64]{0:T(128)S(1)} %get-tuple-element.291, f32[2048]{0:T(1024)S(1)} %copy-done.38), channel_id=1, replica_groups=mesh['dp'=4,'ctx'=8] {'dp','ctx'}, use_global_device_ids=true, to_apply=%region_19.20 | all-reduce | flops 4224 | bytes 33792 | tf_op jit(solution)/shard_map/psum | solution.py:233
  573.5 70.1 %reduce-scatter.10.cloned.1.call-done = f32[32,2048]{1,0:T(8,128)} async-done(((f32[1024,2048]{1,0:T(8,128)}), f32[32,2048]{1,0:T(8,128)}) %reduce-scatter.10.cloned.1.call-update) | async-done | bytes 262160 | tf_op jit(solution)/shard_map/reduce_scatter | solution.py:231
  643.6 147.4 %reduce-scatter.14.cloned.1.call-done = f32[32,2048]{1,0:T(8,128)} async-done(((f32[1024,2048]{1,0:T(8,128)}), f32[32,2048]{1,0:T(8,128)}) %reduce-scatter.14.cloned.1.call-update) | async-done | bytes 262160 | tf_op jit(solution)/shard_map/reduce_scatter | solution.py:160
  791.1 158.8 %reduce-scatter.8.cloned.1.call-done = f32[64,1536]{1,0:T(8,128)} async-done(((f32[2048,1536]{1,0:T(8,128)}), f32[64,1536]{1,0:T(8,128)}) %reduce-scatter.8.cloned.1.call-update) | async-done | bytes 393232 | tf_op jit(solution)/shard_map/reduce_scatter | solution.py:230
  949.8 184.9 %reduce-scatter.12.cloned.1.call-done = f32[64,2048]{1,0:T(8,128)} async-done(((f32[2048,2048]{1,0:T(8,128)}), f32[64,2048]{1,0:T(8,128)}) %reduce-scatter.12.cloned.1.call-update) | async-done | bytes 524304 | tf_op jit(solution)/shard_map/reduce_scatter | solution.py:159
  (415 shorter events, 227.8 us)
Async XLA Ops:
  7.2 75.9 %all-gather.8.cloned.1.call-start = ((), (), s32[]{:S(2)}) async-start(), calls=%async_computation.5 | async-start | bytes 6488064 | tf_op jit(solution)/shard_map/all_gather | solution.py:65
  7.9 103.6 %all-gather.12.cloned.1.call-start = ((), (), s32[]{:S(2)}) async-start(), calls=%async_computation.7 | async-start | bytes 1179648 | tf_op jit(solution)/shard_map/all_gather | solution.py:80
  10.7 72.4 %copy-start.30 = (f32[256]{0:T(256)}, f32[256]{0:T(256)S(1)}, u32[]{:S(2)}) copy-start(f32[256]{0:T(256)S(1)} %fusion.74) | copy-start | bytes 3076
  10.9 77.4 %copy-start.39 = (f32[64]{0:T(128)S(1)}, f32[64]{0:T(128)}, u32[]{:S(2)}) copy-start(f32[64]{0:T(128)} %param.23) | copy-start | bytes 772
  88.1 13.9 %copy-start.15 = (f32[256,1536]{1,0:T(8,128)}, f32[256,1536]{1,0:T(8,128)S(1)}, u32[]{:S(2)}) copy-start(f32[256,1536]{1,0:T(8,128)S(1)} %fusion.67) | copy-start | bytes 4718596
  88.3 13.0 %copy-start.25 = (f32[256,4]{0,1:T(4,128)}, f32[256,4]{0,1:T(4,128)S(1)}, u32[]{:S(2)}) copy-start(f32[256,4]{0,1:T(4,128)S(1)} %multiply_reduce_fusion.9) | copy-start | bytes 12292
  89.3 81.2 %all-gather.10.cloned.1.call-start = ((), (), s32[]{:S(2)}) async-start(), calls=%async_computation.6 | async-start | bytes 1179648 | tf_op jit(solution)/shard_map/all_gather | solution.py:81
  90.2 115.8 %all-gather.14.cloned.1.call-start = ((), (), s32[]{:S(2)}) async-start(), calls=%async_computation.8 | async-start | bytes 4325376 | tf_op jit(solution)/shard_map/all_gather | solution.py:66
  90.7 190.4 %all-gather.16.cloned.1.call-start = ((), (), s32[]{:S(2)}) async-start(), calls=%async_computation.9 | async-start | bytes 8650752 | tf_op jit(solution)/shard_map/all_gather | solution.py:136
  91.3 253.2 %all-gather.18.cloned.1.call-start = ((), (), s32[]{:S(2)}) async-start(), calls=%async_computation.10 | async-start | bytes 4325376 | tf_op jit(solution)/shard_map/all_gather | solution.py:137
  91.9 399.7 %reduce-scatter.6.cloned.1.call-start = ((), (), s32[]{:S(2)}) async-start(), calls=%async_computation.11 | async-start | bytes 2359296 | tf_op jit(solution)/shard_map/reduce_scatter | solution.py:213
  206.0 75.2 %copy-start.27 = (f32[2048]{0:T(1024)S(1)}, f32[2048]{0:T(1024)}, u32[]{:S(2)}) copy-start(f32[2048]{0:T(1024)} %param.25) | copy-start | bytes 24580
  209.9 143.8 %copy-start.7 = (f32[256,2048]{1,0:T(8,128)}, f32[256,2048]{1,0:T(8,128)S(1)}, u32[]{:S(2)}) copy-start(f32[256,2048]{1,0:T(8,128)S(1)} %get-tuple-element.367) | copy-start | bytes 6291460
  209.9 143.8 %copy-start.32 = (f32[256]{0:T(256)}, f32[256]{0:T(256)S(1)}, u32[]{:S(2)}) copy-start(f32[256]{0:T(256)S(1)} %fusion.75) | copy-start | bytes 3076
  451.7 191.9 %reduce-scatter.10.cloned.1.call-start = ((), (), s32[]{:S(2)}) async-start(), calls=%async_computation.13 | async-start | bytes 8650752 | tf_op jit(solution)/shard_map/reduce_scatter | solution.py:231
  457.9 333.1 %reduce-scatter.14.cloned.1.call-start = ((), (), s32[]{:S(2)}) async-start(), calls=%async_computation.15 | async-start | bytes 8650752 | tf_op jit(solution)/shard_map/reduce_scatter | solution.py:160
  464.8 485.1 %reduce-scatter.8.cloned.1.call-start = ((), (), s32[]{:S(2)}) async-start(), calls=%async_computation.12 | async-start | bytes 12976128 | tf_op jit(solution)/shard_map/reduce_scatter | solution.py:230
  469.4 26.9 %copy-start.40 = (f32[64]{0:T(128)S(1)}, f32[64]{0:T(128)}, u32[]{:S(2)}) copy-start(f32[64]{0:T(128)} %param.23) | copy-start | bytes 772
  469.4 27.0 %copy-start.26 = (f32[256,4]{0,1:T(4,128)S(1)}, f32[256,4]{0,1:T(4,128)}, u32[]{:S(2)}) copy-start(f32[256,4]{0,1:T(4,128)} %copy-done.25) | copy-start | bytes 12292
  471.9 26.4 %copy-start.8 = (bf16[1,256,2048]{2,1,0:T(8,128)(2,1)S(1)}, bf16[1,256,2048]{2,1,0:T(8,128)(2,1)}, u32[]{:S(2)}) copy-start(bf16[1,256,2048]{2,1,0:T(8,128)(2,1)} %param.17) | copy-start | bytes 3145732
  471.9 26.4 %copy-start.24 = (f32[2048]{0:T(1024)S(1)}, f32[2048]{0:T(1024)}, u32[]{:S(2)}) copy-start(f32[2048]{0:T(1024)} %param.20) | copy-start | bytes 24580
  471.9 26.4 %copy-start.31 = (f32[256]{0:T(256)S(1)}, f32[256]{0:T(256)}, u32[]{:S(2)}) copy-start(f32[256]{0:T(256)} %copy-done.30) | copy-start | bytes 3076
  506.1 628.6 %reduce-scatter.12.cloned.1.call-start = ((), (), s32[]{:S(2)}) async-start(), calls=%async_computation.14 | async-start | bytes 17301504 | tf_op jit(solution)/shard_map/reduce_scatter | solution.py:159
  522.8 47.6 %copy-start.37 = (f32[256]{0:T(256)S(1)}, f32[256]{0:T(256)}, u32[]{:S(2)}) copy-start(f32[256]{0:T(256)} %copy-done.36) | copy-start | bytes 3076
  (66 other events, 166.7 us)
Sparse Core Ops, SparseCore 0:
  10.9 72.1 all-gather.7
  89.4 22.0 all-gather.11
  114.0 23.5 all-gather.9
  140.3 62.0 all-gather.13
  205.1 76.0 all-gather.15
  283.9 60.6 all-gather.17
  451.9 39.7 reduce-scatter.5
  494.6 148.9 reduce-scatter.9
  646.6 144.4 reduce-scatter.13
  798.5 151.2 reduce-scatter.7
  952.7 181.9 reduce-scatter.11
where the time goes:
time: 1140 us
  waiting for transfers between devices  788 us (69%)
  matrix products  201 us (18%)
  blocking collectives  50.3 us (4%)
  other arithmetic  45.7 us (4%)
  local copies, waits for them, and re-layouts  39.5 us (3%)
  between operations  14.4 us (1%)
    reduce_scatter x1, waiting for transfers between devices, per_device(): lax.psum_scatter(grad_gateup, ('dp', 'ctx'), scatter_dimension=0, tiled=T...  185 us
    reduce_scatter x1, waiting for transfers between devices, per_device(): lax.psum_scatter(grad_qkv_w, ('dp', 'ctx'), scatter_dimension=0, tiled=True)  159 us
    reduce_scatter x1, waiting for transfers between devices, per_device(): lax.psum_scatter(grad_down, ('dp', 'ctx'), scatter_dimension=0, tiled=True)  147 us
    all_gather x1, waiting for transfers between devices, per_device(): lax.all_gather(w_qkv, ('dp', 'ctx'), axis=0, tiled=True)  72.2 us
    all_gather x1, waiting for transfers between devices, per_device(): lax.all_gather(w_gateup, ('dp', 'ctx'), axis=0, tiled=True)  71.3 us
    reduce_scatter x1, waiting for transfers between devices, per_device(): lax.psum_scatter(grad_out_w, ('dp', 'ctx'), scatter_dimension=0, tiled=True)  70.1 us
    all_gather x1, waiting for transfers between devices, per_device(): lax.all_gather(w_down, ('dp', 'ctx'), axis=0, tiled=True)  56.3 us
    dot_general x16, matrix products, score_block(): jnp.einsum('igrd,jgd->grij', query_b, key_blk, preferred_element_type=jnp...  42.2 us
  transfers between devices with their start and end apart: 11, of which 9 were waited for; matrix products, arithmetic and copies ran while one was open for 15% of the time, Pallas kernels for 0%

commit v1 on v0

--- a/solution.py
+++ b/solution.py
@@ -1,9 +1,446 @@
+import functools
 import math
 
 import jax
 import jax.numpy as jnp
 from jax import lax
+from jax.experimental import pallas as pl
+from jax.experimental.pallas import tpu as pltpu
 from jax.sharding import PartitionSpec as P
+MESH = pl.DeviceIdType.MESH
+NZ = 4
+ZT=[0,1,2,3]
+PT=[1.5,2.5,4,5.5]
+CT=[3.5,5.2,6.2,7.2]
+
+class Place:
+    def __init__(self):
+        self.z = lax.axis_index("dp")
+        c = lax.axis_index("ctx")
+        self.core = c % 2
+        self.x = (c // 2) % 2
+        self.y = c // 4
+    def at(self, z=None, y=None, x=None, core=None):
+        z = self.z if z is None else z
+        y = self.y if y is None else y
+        x = self.x if x is None else x
+        core = self.core if core is None else core
+        return (z, y * 4 + x * 2 + core)
+    def xn(self): return self.at(x=1 - self.x)
+    def yn(self): return self.at(y=1 - self.y)
+    def sn(self): return self.at(core=1 - self.core)
+    def up(self): return self.at(z=self.z + 1)
+    def down(self): return self.at(z=self.z - 1)
+
+def barrier(pc):
+    bar = pltpu.get_barrier_semaphore()
+    sig = lambda d: pl.semaphore_signal(bar, inc=1, device_id=d, device_id_type=MESH)
+    for d in (pc.xn(), pc.yn(), pc.sn()): sig(d)
+    @pl.when(pc.z < NZ - 1)
+    def _(): sig(pc.up())
+    @pl.when(pc.z > 0)
+    def _(): sig(pc.down())
+    pl.semaphore_wait(bar, 3 + (1 - pc.z // (NZ - 1)) + (pc.z + NZ - 1) // NZ)
+
+KZ, KX, KY, KD0, KD1, KS = range(6)
+KU = 6
+
+class Gather:
+    def __init__(self, pc, buf, send, recv):
+        self.pc, self.buf, self.send, self.recv = pc, buf, send, recv
+        R = buf.shape[-2]
+        self.h = (pl.ds(0, R // 2), pl.ds(R // 2, R // 2))
+    def cp(self, idx, dev, ks, kr, slot):
+        ref = self.buf.at[idx]
+        return pltpu.make_async_remote_copy(src_ref=ref, dst_ref=ref, send_sem=self.send.at[ks, slot], recv_sem=self.recv.at[kr, slot], device_id=dev, device_id_type=MESH)
+    def c_up(self, z0): p = self.pc; return self.cp((z0, p.y, p.x, p.core), p.up(), KU, KZ, z0)
+    def c_down(self, z0): p = self.pc; return self.cp((z0, p.y, p.x, p.core), p.down(), KZ, KZ, z0)
+    def c_x(self, z0): p = self.pc; return self.cp((z0, p.y, p.x, p.core), p.xn(), KX, KX, z0)
+    def c_y(self, z0): p = self.pc; return self.cp((z0, p.y, p.x, p.core), p.yn(), KY, KY, z0)
+    def c_d0(self, z0): p = self.pc; return self.cp((z0, p.y, 1 - p.x, p.core, self.h[0]), p.yn(), KD0, KD0, z0)
+    def c_d1(self, z0): p = self.pc; return self.cp((z0, 1 - p.y, p.x, p.core, self.h[1]), p.xn(), KD1, KD1, z0)
+    def c_s(self, z0): p = self.pc; return self.cp((z0, slice(None), slice(None), p.core), p.sn(), KS, KS, z0)
+    def plane_send(self, z0):
+        self.c_x(z0).start(); self.c_y(z0).start()
+    def own(self):
+        z = self.pc.z
+        @pl.when(z < NZ - 1)
+        def _(): self.c_up(z).start()
+        @pl.when(z > 0)
+        def _(): self.c_down(z).start()
+        self.plane_send(z)
+    def z_event(self, s, below):
+        z = self.pc.z
+        if below:
+            z0 = z - s
+            @pl.when(z0 >= 0)
+            def _():
+                self.c_up(z0).wait_recv()
+                @pl.when(z < NZ - 1)
+                def _(): self.c_up(z0).start()
+                self.plane_send(z0)
+        else:
+            z0 = z + s
+            @pl.when(z0 < NZ)
+            def _():
+                self.c_down(z0).wait_recv()
+                @pl.when(z > 0)
+                def _(): self.c_down(z0).start()
+                self.plane_send(z0)
+    def plane_event(self, z0):
+        self.c_x(z0).wait_recv()
+        self.c_d0(z0).start()
+        self.c_y(z0).wait_recv()
+        self.c_d1(z0).start()
+    def core_event(self, z0):
+        self.c_d0(z0).wait_recv()
+        self.c_d1(z0).wait_recv()
+        self.c_s(z0).start()
+    def done_event(self, z0):
+        self.c_s(z0).wait_recv()
+    def finish(self):
+        z = self.pc.z
+        for z0 in range(NZ):
+            for c in (self.c_x, self.c_y, self.c_d0, self.c_d1, self.c_s):
+                c(z0).wait_send()
+            @pl.when((z < NZ - 1) & (z0 <= z))
+            def _(): self.c_up(z0).wait_send()
+            @pl.when((z > 0) & (z0 >= z))
+            def _(): self.c_down(z0).wait_send()
+
+
+class GatherPlane:
+    def __init__(self, pc, buf, send, recv):
+        self.pc, self.buf, self.send, self.recv = pc, buf, send, recv
+        R = buf.shape[-2]
+        self.h = (pl.ds(0, R // 2), pl.ds(R // 2, R // 2))
+    def cp(self, idx, dev, s, r):
+        ref = self.buf.at[idx]
+        return pltpu.make_async_remote_copy(src_ref=ref, dst_ref=ref, send_sem=self.send.at[s], recv_sem=self.recv.at[r], device_id=dev, device_id_type=MESH)
+    def yx(self, k):
+        p = self.pc
+        return (p.y if k < 2 else 1 - p.y), (p.x if k % 2 == 0 else 1 - p.x)
+    def kk(self, y, x): return y * 2 + x
+    def c_x(self): p = self.pc; return self.cp((p.z, p.y, p.x, p.core), p.xn(), (KX, 0), (KX, 0))
+    def c_y(self): p = self.pc; return self.cp((p.z, p.y, p.x, p.core), p.yn(), (KY, 0), (KY, 0))
+    def c_d0(self): p = self.pc; return self.cp((p.z, p.y, 1 - p.x, p.core, self.h[0]), p.yn(), (KD0, 0), (KD0, 0))
+    def c_d1(self): p = self.pc; return self.cp((p.z, 1 - p.y, p.x, p.core, self.h[1]), p.xn(), (KD1, 0), (KD1, 0))
+    def c_up(self, z0, k): p = self.pc; y, x = self.yx(k); return self.cp((z0, y, x, p.core), p.up(), (KZ + 10 + z0, k), (KZ + 10 + z0, k))
+    def c_down(self, z0, k): p = self.pc; y, x = self.yx(k); return self.cp((z0, y, x, p.core), p.down(), (14 + z0, k), (KZ + 10 + z0, k))
+    def c_s(self, z0): p = self.pc; return self.cp((z0, slice(None), slice(None), p.core), p.sn(), (KS, z0), (KS, z0))
+    def z_send(self, k):
+        z = self.pc.z
+        @pl.when(z < NZ - 1)
+        def _(): self.c_up(z, k).start()
+        @pl.when(z > 0)
+        def _(): self.c_down(z, k).start()
+    def own(self):
+        self.c_x().start(); self.c_y().start()
+        self.z_send(0)
+    def plane_event(self):
+        self.c_x().wait_recv(); self.c_d0().start()
+        self.z_send(1)
+        self.c_y().wait_recv(); self.c_d1().start()
+        self.z_send(2)
+    def diag_event(self):
+        self.c_d0().wait_recv(); self.c_d1().wait_recv()
+        self.z_send(3)
+        self.c_s(self.pc.z).start()
+    def z_event(self, s, k):
+        z = self.pc.z
+        @pl.when(z - s >= 0)
+        def _():
+            c = self.c_up(z - s, k); c.wait_recv()
+            @pl.when(z < NZ - 1)
+            def _(): c.start()
+        @pl.when(z + s < NZ)
+        def _():
+            c = self.c_down(z + s, k); c.wait_recv()
+            @pl.when(z > 0)
+            def _(): c.start()
+    def core_event(self, s):
+        z = self.pc.z
+        @pl.when(z - s >= 0)
+        def _(): self.c_s(z - s).start()
+        @pl.when(z + s < NZ)
+        def _(): self.c_s(z + s).start()
+    def done_event(self, z0):
+        self.c_s(z0).wait_recv()
+    def finish(self):
+        z = self.pc.z
+        for c in (self.c_x, self.c_y, self.c_d0, self.c_d1): c().wait_send()
+        for z0 in range(NZ):
+            self.c_s(z0).wait_send()
+            for k in range(4):
+                @pl.when((z < NZ - 1) & (z0 <= z))
+                def _(): self.c_up(z0, k).wait_send()
+                @pl.when((z > 0) & (z0 >= z))
+                def _(): self.c_down(z0, k).wait_send()
+
+def near(z, i):
+    return None
+
+def ag_kernel(n, W, plane_first, *refs):
+    ins, outs = refs[:n], refs[n:2 * n]
+    send, recv, lsem = refs[2 * n:]
+    pc = Place()
+    loc = [pltpu.make_async_copy(i, o.at[pc.z, pc.y, pc.x, pc.core], lsem.at[k]) for k, (i, o) in enumerate(zip(ins, outs))]
+    for l in loc: l.start()
+    barrier(pc)
+    for l in loc: l.wait()
+    z = pc.z
+    ev = []
+    gs = []
+    def both(fn, s):
+        if s == 0:
+            fn(z)
+        else:
+            @pl.when(z - s >= 0)
+            def _(): fn(z - s)
+            @pl.when(z + s < NZ)
+            def _(): fn(z + s)
+    for k, o in enumerate(outs):
+        T = W[k]
+        if k in plane_first:
+            g = GatherPlane(pc, o, send.at[k], recv.at[k]); gs.append(g)
+            ev.append((T, g.own))
+            ev.append((T + 1, g.plane_event)); ev.append((T + 2, g.diag_event))
+            for s in range(1, NZ):
+                for j in range(4):
+                    ev.append((T + s * 2 + j * 0.5, functools.partial(g.z_event, s, j)))
+                ev.append((T + s * 2 + 2.1, functools.partial(g.core_event, s)))
+        else:
+            g = Gather(pc, o, send.at[k], recv.at[k]); gs.append(g)
+            ev.append((T, g.own))
+            for s in range(1, NZ):
+                ev.append((T + ZT[s], functools.partial(g.z_event, s, True)))
+                ev.append((T + ZT[s], functools.partial(g.z_event, s, False)))
+            for s in range(NZ):
+                ev.append((T + PT[s], functools.partial(both, g.plane_event, s)))
+                ev.append((T + CT[s], functools.partial(both, g.core_event, s)))
+    ev.sort(key=lambda e: e[0])
+    for _, e in ev: e()
+    for g in gs:
+        for z0 in range(NZ): g.done_event(z0)
+    for g in gs: g.finish()
+
+def gather_all(shards, W=(0,0,0,0), plane_first=()):
+    n = len(shards)
+    outs = [jax.ShapeDtypeStruct((NZ, 2, 2, 2) + s.shape, s.dtype) for s in shards]
+    res = pl.pallas_call(functools.partial(ag_kernel, n, W, plane_first), out_shape=outs,
+        in_specs=[pl.BlockSpec(memory_space=pl.ANY)] * n, out_specs=[pl.BlockSpec(memory_space=pl.ANY)] * n,
+        scratch_shapes=[pltpu.SemaphoreType.DMA((n, 18, NZ)), pltpu.SemaphoreType.DMA((n, 14, NZ)), pltpu.SemaphoreType.DMA((n,))],
+        compiler_params=pltpu.CompilerParams(collective_id=0, has_side_effects=True), name="gather_weights")(*shards)
+    return res
+
+f32 = jnp.float32
+bf16 = jnp.bfloat16
+
+def far(z, i):
+    m = z // 2
+    zz = z + m * (3 - 2 * z)
+    lo = 3 - i if i < 2 else (1 - zz if i == 2 else zz)
+    return lo + m * (3 - 2 * lo)
+
+SD0, SD1, SX0, SX1, SY0, SY1, SA, SB = range(8)
+
+class Scatter:
+    def __init__(self, pc, part, bufs, out, send, recv):
+        self.pc, self.part, self.out, self.send, self.recv = pc, part, out, send, recv
+        self.rd, self.rx, self.ry, self.za, self.zb, self.sm = bufs
+        R = part.shape[-2]
+        self.R = R
+        self.h = (pl.ds(0, R // 2), pl.ds(R // 2, R // 2))
+    def cp(self, src, dst, dev, k, zp):
+        return pltpu.make_async_remote_copy(src_ref=src, dst_ref=dst, send_sem=self.send.at[k, zp], recv_sem=self.recv.at[k, zp], device_id=dev, device_id_type=MESH)
+    def d0(self, zp): p = self.pc; return self.cp(self.part.at[zp, 1 - p.y, 1 - p.x, self.h[0]], self.rd.at[zp, 0], p.yn(), SD0, zp)
+    def d1(self, zp): p = self.pc; return self.cp(self.part.at[zp, 1 - p.y, 1 - p.x, self.h[1]], self.rd.at[zp, 1], p.xn(), SD1, zp)
+    def x1(self, zp): p = self.pc; return self.cp(self.part.at[zp, p.y, 1 - p.x, self.h[1]], self.rx.at[zp, 1], p.xn(), SX1, zp)
+    def y0(self, zp): p = self.pc; return self.cp(self.part.at[zp, 1 - p.y, p.x, self.h[0]], self.ry.at[zp, 0], p.yn(), SY0, zp)
+    def x0(self, zp): p = self.pc; return self.cp(self.rd.at[zp, 0], self.rx.at[zp, 0], p.xn(), SX0, zp)
+    def y1(self, zp): p = self.pc; return self.cp(self.rd.at[zp, 1], self.ry.at[zp, 1], p.yn(), SY1, zp)
+    def down(self, zp): p = self.pc; return self.cp(self.sm.at[zp], self.za.at[zp], p.down(), SA, zp)
+    def up(self, zp): p = self.pc; return self.cp(self.sm.at[zp], self.zb.at[zp], p.up(), SB, zp)
+    def first(self, i):
+        zp = far(self.pc.z, i)
+        for c in (self.d0, self.d1, self.x1, self.y0): c(zp).start()
+    def d_event(self, i):
+        p = self.pc; zp = far(p.z, i)
+        self.d0(zp).wait_recv()
+        self.rd[zp, 0] = self.rd[zp, 0] + self.part[zp, p.y, 1 - p.x, self.h[0]]
+        self.x0(zp).start()
+        self.d1(zp).wait_recv()
+        self.rd[zp, 1] = self.rd[zp, 1] + self.part[zp, 1 - p.y, p.x, self.h[1]]
+        self.y1(zp).start()
+    def xy_event(self, i):
+        p = self.pc; zp = far(p.z, i)
+        for c in (self.x1, self.y0, self.x0, self.y1): c(zp).wait_recv()
+        for k in range(2):
+            self.sm[zp, self.h[k]] = (self.part[zp, p.y, p.x, self.h[k]].astype(f32) + self.rx[zp, k].astype(f32) + self.ry[zp, k].astype(f32)).astype(bf16)
+    def z_event(self, i):
+        z = self.pc.z; zp = far(z, i)
+        @pl.when(zp < z)
+        def _():
+            @pl.when(z < NZ - 1)
+            def _():
+                self.down(zp).wait_recv()
+                self.sm[zp] = self.sm[zp] + self.za[zp]
+            self.down(zp).start()
+        @pl.when(zp > z)
+        def _():
+            @pl.when(z > 0)
+            def _():
+                self.up(zp).wait_recv()
+                self.sm[zp] = self.sm[zp] + self.zb[zp]
+            self.up(zp).start()
+    def final(self):
+        p = self.pc; z = p.z
+        for c in (self.x1, self.y0, self.x0, self.y1): c(z).wait_recv()
+        for k in range(2):
+            self.out[self.h[k], :] = self.part[z, p.y, p.x, self.h[k]].astype(f32) + self.rx[z, k].astype(f32) + self.ry[z, k].astype(f32)
+        @pl.when(z < NZ - 1)
+        def _():
+            self.down(z).wait_recv()
+            self.out[...] += self.za[z].astype(f32)
+        @pl.when(z > 0)
+        def _():
+            self.up(z).wait_recv()
+            self.out[...] += self.zb[z].astype(f32)
+    def finish(self):
+        z = self.pc.z
+        for zp in range(NZ):
+            for c in (self.d0, self.d1, self.x1, self.y0, self.x0, self.y1): c(zp).wait_send()
+            @pl.when(zp < z)
+            def _(): self.down(zp).wait_send()
+            @pl.when(zp > z)
+            def _(): self.up(zp).wait_send()
+    @staticmethod
+    def scratch(R, C):
+        v = pltpu.VMEM
+        return [v((NZ, 2, R // 2, C), bf16), v((NZ, 2, R // 2, C), bf16), v((NZ, 2, R // 2, C), bf16), v((NZ, R, C), bf16), v((NZ, R, C), bf16), v((NZ, R, C), bf16)]
+
+class ScatterZ:
+    def __init__(self, pc, part, bufs, out, send, recv):
+        self.pc, self.part, self.out, self.send, self.recv = pc, part, out, send, recv
+        self.rd, self.rx, self.ry, self.za, self.zb, self.sm = bufs
+        R = part.shape[-2]
+        self.h = (pl.ds(0, R // 2), pl.ds(R // 2, R // 2))
+    def cp(self, src, dst, dev, k, s):
+        return pltpu.make_async_remote_copy(src_ref=src, dst_ref=dst, send_sem=self.send.at[k, s], recv_sem=self.recv.at[k, s], device_id=dev, device_id_type=MESH)
+    def yx(self, k): return k // 2, k % 2
+    def down(self, zp, k, src): return self.cp(src, self.za.at[zp, k], self.pc.down(), 8 + zp, k)
+    def up(self, zp, k, src): return self.cp(src, self.zb.at[zp, k], self.pc.up(), 12 + zp, k)
+    def first(self, i):
+        z = self.pc.z; zp = far(z, i)
+        for k in range(4):
+            y, x = self.yx(k)
+            @pl.when((z == NZ - 1) & (zp < z))
+            def _(): self.down(zp, k, self.part.at[zp, y, x]).start()
+            @pl.when((z == 0) & (zp > z))
+            def _(): self.up(zp, k, self.part.at[zp, y, x]).start()
+    def z_event(self, i, k):
+        z = self.pc.z; zp = far(z, i); y, x = self.yx(k)
+        @pl.when((zp < z) & (z < NZ - 1))
+        def _():
+            self.down(zp, k, self.za.at[zp, k]).wait_recv()
+            self.za[zp, k] = self.za[zp, k] + self.part[zp, y, x]
+            self.down(zp, k, self.za.at[zp, k]).start()
+        @pl.when((zp > z) & (z > 0))
+        def _():
+            self.up(zp, k, self.zb.at[zp, k]).wait_recv()
+            self.zb[zp, k] = self.zb[zp, k] + self.part[zp, y, x]
+            self.up(zp, k, self.zb.at[zp, k]).start()
+    def own_event(self, k):
+        z = self.pc.z; y, x = self.yx(k)
+        @pl.when(z < NZ - 1)
+        def _(): self.down(z, k, self.za.at[z, k]).wait_recv()
+        @pl.when(z > 0)
+        def _(): self.up(z, k, self.zb.at[z, k]).wait_recv()
+        @pl.when(z == 0)
+        def _(): self.sm[k] = self.part[z, y, x] + self.za[z, k]
+        @pl.when(z == NZ - 1)
+        def _(): self.sm[k] = self.part[z, y, x] + self.zb[z, k]
+        @pl.when((z > 0) & (z < NZ - 1))
+        def _(): self.sm[k] = (self.part[z, y, x].astype(f32) + self.za[z, k].astype(f32) + self.zb[z, k].astype(f32)).astype(bf16)
+    def kk(self, y, x): return y * 2 + x
+    def d0(self): p = self.pc; return self.cp(self.sm.at[self.kk(1 - p.y, 1 - p.x), self.h[0]], self.rd.at[0, 0], p.yn(), SD0, 0)
+    def d1(self): p = self.pc; return self.cp(self.sm.at[self.kk(1 - p.y, 1 - p.x), self.h[1]], self.rd.at[0, 1], p.xn(), SD1, 0)
+    def x1(self): p = self.pc; return self.cp(self.sm.at[self.kk(p.y, 1 - p.x), self.h[1]], self.rx.at[0, 1], p.xn(), SX1, 0)
+    def y0(self): p = self.pc; return self.cp(self.sm.at[self.kk(1 - p.y, p.x), self.h[0]], self.ry.at[0, 0], p.yn(), SY0, 0)
+    def x0(self): p = self.pc; return self.cp(self.rd.at[0, 0], self.rx.at[0, 0], p.xn(), SX0, 0)
+    def y1(self): p = self.pc; return self.cp(self.rd.at[0, 1], self.ry.at[0, 1], p.yn(), SY1, 0)
+    def plane_send(self):
+        for c in (self.d0, self.d1, self.x1, self.y0): c().start()
+    def plane_event(self):
+        p = self.pc
+        self.d0().wait_recv()
+        self.rd[0, 0] = self.rd[0, 0] + self.sm[self.kk(p.y, 1 - p.x), self.h[0]]
+        self.x0().start()
+        self.d1().wait_recv()
+        self.rd[0, 1] = self.rd[0, 1] + self.sm[self.kk(1 - p.y, p.x), self.h[1]]
+        self.y1().start()
+    def final(self):
+        p = self.pc
+        for c in (self.x1, self.y0, self.x0, self.y1): c().wait_recv()
+        for k in range(2):
+            self.out[self.h[k], :] = self.sm[self.kk(p.y, p.x), self.h[k]].astype(f32) + self.rx[0, k].astype(f32) + self.ry[0, k].astype(f32)
+    def finish(self):
+        z = self.pc.z
+        for c in (self.d0, self.d1, self.x1, self.y0, self.x0, self.y1): c().wait_send()
+        for zp in range(NZ):
+            for k in range(4):
+                @pl.when(zp < z)
+                def _(): self.down(zp, k, self.za.at[zp, k]).wait_send()
+                @pl.when(zp > z)
+                def _(): self.up(zp, k, self.zb.at[zp, k]).wait_send()
+    @staticmethod
+    def scratch(R, C):
+        v = pltpu.VMEM
+        return [v((1, 2, R // 2, C), bf16), v((1, 2, R // 2, C), bf16), v((1, 2, R // 2, C), bf16), v((NZ, 4, R, C), bf16), v((NZ, 4, R, C), bf16), v((4, R, C), bf16)]
+
+FT=[0,0,0,0]; DT=[1,2,3,4]; XT=[2.2,3.2,4.2,5.2]; RZT=[2.5,3.5,4.5]; FINAL=6
+def rs_kernel(n, W, zfirst, *refs):
+    ins, outs = refs[:n], refs[n:2 * n]
+    send, recv = refs[2 * n:2 * n + 2]
+    bufs = refs[2 * n + 2:]
+    pc = Place()
+    barrier(pc)
+    ev = []; gs = []
+    P_ = functools.partial
+    for k in range(n):
+        b = bufs[6 * k:6 * k + 6]; T = W[k]
+        cls = ScatterZ if k in zfirst else Scatter
+        g = cls(pc, ins[k], b, outs[k], send.at[k], recv.at[k]); gs.append(g)
+        if k in zfirst:
+            for i in range(3):
+                ev.append((T, P_(g.first, i)))
+                for j in range(4): ev.append((T + 0.5 + i + j * .25, P_(g.z_event, i, j)))
+            for j in range(4): ev.append((T + 4 + j * .01, P_(g.own_event, j)))
+            ev.append((T + 4.1, g.plane_send)); ev.append((T + 5, g.plane_event)); ev.append((T + 6.5, g.final))
+        else:
+            for i in range(4):
+                ev.append((T + FT[i], P_(g.first, i)))
+                ev.append((T + DT[i], P_(g.d_event, i)))
+                if i < 3:
+                    ev.append((T + XT[i], P_(g.xy_event, i)))
+                    ev.append((T + RZT[i], P_(g.z_event, i)))
+            ev.append((T + FINAL, g.final))
+    ev.sort(key=lambda e: e[0])
+    for _, e in ev: e()
+    for g in gs: g.finish()
+
+def scatter_all(parts, W=(0, 0, 0, 0), zfirst=()):
+    n = len(parts)
+    outs = [jax.ShapeDtypeStruct(s.shape[-2:], f32) for s in parts]
+    scr = []
+    for k, s in enumerate(parts):
+        scr += (ScatterZ if k in zfirst else Scatter).scratch(*s.shape[-2:])
+    V = pl.BlockSpec(memory_space=pltpu.VMEM)
+    return pl.pallas_call(functools.partial(rs_kernel, n, W, zfirst), out_shape=outs,
+        in_specs=[V] * n, out_specs=[V] * n,
+        scratch_shapes=[pltpu.SemaphoreType.DMA((n, 16, NZ)), pltpu.SemaphoreType.DMA((n, 16, NZ))] + scr,
+        compiler_params=pltpu.CompilerParams(collective_id=1, has_side_effects=True, vmem_limit_bytes=60 << 20), name="scatter_grads")(*parts)
+
 
 HEADS = 16
 GROUPS = 4
@@ -53,7 +490,7 @@
     return jax.nn.silu(gate_up[:, :FF]) * gate_up[:, FF:]
 
 
-def per_device(
+def per_device_plain(
     inputs, places, cotangent, attn_gain, w_qkv, q_gain, k_gain, w_out, ffn_gain, w_gateup, w_down
 ):
     tok_rows = inputs.shape[1]
@@ -229,6 +666,195 @@
     grad_qkv_own, grad_out_own = (
         lax.psum_scatter(grad_qkv_w, ("dp", "ctx"), scatter_dimension=0, tiled=True),
         lax.psum_scatter(grad_out_w, ("dp", "ctx"), scatter_dimension=0, tiled=True),
+    )
+    gain_attn, gain_query, gain_key, gain_ffn = lax.psum(
+        (grad_attn_gain, grad_q_gain, grad_k_gain, grad_ffn_gain), ("dp", "ctx")
+    )
+    return (
+        layer_output,
+        grad_inputs,
+        gain_attn,
+        grad_qkv_own,
+        gain_query,
+        gain_key,
+        grad_out_own,
+        gain_ffn,
+        grad_gateup_own,
+        grad_down_own,
+    )
+
+
+def per_device_fast(
+    inputs, places, cotangent, attn_gain, w_qkv, q_gain, k_gain, w_out, ffn_gain, w_gateup, w_down
+):
+    tok_rows = inputs.shape[1]
+    repeat = HEADS // GROUPS
+    score_scale = HEAD_DIM ** (-0.5)
+    here_f = inputs[0].astype(jnp.float32)
+    own_places = places[0]
+    qkv_w, out_w, gateup_w, down_w = [
+        w.reshape(-1, w.shape[-1])
+        for w in gather_all((w_qkv, w_out, w_gateup, w_down), plane_first=(1,))
+    ]
+    core = lax.axis_index("ctx") % 2
+
+    def both(array):
+        other = lax.ppermute(array, "ctx", [(i, i ^ 1) for i in range(lax.axis_size("ctx"))])
+        return jnp.concatenate([array, other], axis=0)
+
+    def grad_half(left, right, rows):
+        left = both(left).reshape(2 * tok_rows, -1, 2, rows)
+        left = lax.dynamic_index_in_dim(left, core, 2, keepdims=False).reshape(2 * tok_rows, -1)
+        grad = jnp.dot(left.T, both(right), preferred_element_type=jnp.float32)
+        return grad.astype(jnp.bfloat16).reshape(NZ, 2, 2, rows, right.shape[-1])
+
+    h_attn_f, pull_attn = jax.vjp(norm_rows, here_f, attn_gain)
+    h_attn = h_attn_f.astype(jnp.bfloat16)
+    qkv_all = jnp.dot(h_attn, qkv_w, preferred_element_type=jnp.float32)
+
+    def heads_of(qkv_in, gain_q, gain_k):
+        return project_heads(qkv_in, own_places, gain_q, gain_k)
+
+    (queries, keys_f, values), pull_heads = jax.vjp(heads_of, qkv_all, q_gain, k_gain)
+    query_b = queries.astype(jnp.bfloat16).reshape(tok_rows, GROUPS, repeat, HEAD_DIM)
+    key_b = keys_f.astype(jnp.bfloat16)
+    value_b = values.astype(jnp.bfloat16)
+    all_keys, all_values = (
+        lax.all_gather(key_b, "ctx", axis=0, tiled=True),
+        lax.all_gather(value_b, "ctx", axis=0, tiled=True),
+    )
+    all_places = lax.all_gather(own_places, "ctx", axis=0, tiled=True)
+    blocks = lax.axis_size("ctx")
+    key_blocks = all_keys.reshape(blocks, tok_rows, GROUPS, HEAD_DIM)
+    value_blocks = all_values.reshape(blocks, tok_rows, GROUPS, HEAD_DIM)
+    place_blocks = all_places.reshape(blocks, tok_rows)
+
+    def score_block(key_blk, place_blk):
+        scores = (
+            jnp.einsum("igrd,jgd->grij", query_b, key_blk, preferred_element_type=jnp.float32)
+            * score_scale
+        )
+        allowed = place_blk[None, :] <= own_places[:, None]
+        return (scores, allowed)
+
+    def max_step(state_pair, entries):
+        row_top, row_total = state_pair
+        scores, allowed = score_block(entries[0], entries[1])
+        scores = jnp.where(allowed, scores, -1e30)
+        new_top = jnp.maximum(row_top, jnp.max(scores, axis=-1))
+        row_total = row_total * jnp.exp(row_top - new_top) + jnp.sum(
+            jnp.where(allowed, jnp.exp(scores - new_top[..., None]), 0.0), axis=-1
+        )
+        return ((new_top, row_total), None)
+
+    start_pair = (
+        jnp.full((GROUPS, repeat, tok_rows), -1e30, jnp.float32),
+        jnp.zeros((GROUPS, repeat, tok_rows), jnp.float32),
+    )
+    (row_top, row_total), _ = lax.scan(max_step, start_pair, (key_blocks, place_blocks))
+    log_total = row_top + jnp.log(row_total)
+
+    def out_step(accum, entries):
+        scores, allowed = score_block(entries[0], entries[1])
+        weights_b = jnp.where(allowed, jnp.exp(scores - log_total[..., None]), 0.0).astype(
+            jnp.bfloat16
+        )
+        return (
+            accum
+            + jnp.einsum(
+                "grij,jgd->igrd", weights_b, entries[2], preferred_element_type=jnp.float32
+            ),
+            None,
+        )
+
+    mixed_f, _ = lax.scan(
+        out_step,
+        jnp.zeros((tok_rows, GROUPS, repeat, HEAD_DIM), jnp.float32),
+        (key_blocks, place_blocks, value_blocks),
+    )
+    mixed_b = mixed_f.reshape(tok_rows, HEADS * HEAD_DIM).astype(jnp.bfloat16)
+    attn_out = jnp.dot(mixed_b, out_w, preferred_element_type=jnp.float32)
+    residual = here_f + attn_out
+    h_ffn_f, pull_ffn = jax.vjp(norm_rows, residual, ffn_gain)
+    h_ffn = h_ffn_f.astype(jnp.bfloat16)
+    gate_up = jnp.dot(h_ffn, gateup_w, preferred_element_type=jnp.float32)
+    act_f, pull_gate = jax.vjp(gated, gate_up)
+    act_b = act_f.astype(jnp.bfloat16)
+    result = residual + jnp.dot(act_b, down_w, preferred_element_type=jnp.float32)
+    layer_output = result.astype(jnp.bfloat16)[None]
+    grad_out = cotangent[0]
+    grad_act = jnp.dot(grad_out, down_w.T, preferred_element_type=jnp.float32)
+    grad_down = grad_half(act_b, grad_out, w_down.shape[0])
+    grad_gu_b = pull_gate(grad_act)[0].astype(jnp.bfloat16)
+    grad_gateup = grad_half(h_ffn, grad_gu_b, w_gateup.shape[0])
+    grad_h_ffn = jnp.dot(grad_gu_b, gateup_w.T, preferred_element_type=jnp.float32)
+    grad_resid_part, grad_ffn_gain = pull_ffn(grad_h_ffn)
+    grad_residual = grad_out.astype(jnp.float32) + grad_resid_part
+    grad_attn_b = grad_residual.astype(jnp.bfloat16)
+    grad_out_w = grad_half(mixed_b, grad_attn_b, w_out.shape[0])
+    grad_mixed_b = (
+        jnp.dot(grad_attn_b, out_w.T, preferred_element_type=jnp.float32)
+        .astype(jnp.bfloat16)
+        .reshape(tok_rows, GROUPS, repeat, HEAD_DIM)
+    )
+    row_delta = jnp.transpose(
+        jnp.sum(grad_mixed_b.astype(jnp.float32) * mixed_f, axis=-1), (1, 2, 0)
+    )
+
+    def back_step(grad_query, entries):
+        key_blk, place_blk, value_blk = entries
+        scores, allowed = score_block(key_blk, place_blk)
+        weights_f = jnp.where(allowed, jnp.exp(scores - log_total[..., None]), 0.0)
+        weights_b = weights_f.astype(jnp.bfloat16)
+        grad_value = jnp.einsum(
+            "grij,igrd->jgd", weights_b, grad_mixed_b, preferred_element_type=jnp.float32
+        )
+        grad_prob = jnp.einsum(
+            "igrd,jgd->grij", grad_mixed_b, value_blk, preferred_element_type=jnp.float32
+        )
+        grad_score = (weights_f * (grad_prob - row_delta[..., None])).astype(jnp.bfloat16)
+        grad_query = grad_query + jnp.einsum(
+            "grij,jgd->igrd", grad_score, key_blk, preferred_element_type=jnp.float32
+        )
+        grad_key = (
+            jnp.einsum("grij,igrd->jgd", grad_score, query_b, preferred_element_type=jnp.float32)
+            * score_scale
+        )
+        return (
+            grad_query,
+            jnp.concatenate(
+                [
+                    grad_key.reshape(tok_rows, GROUPS * HEAD_DIM),
+                    grad_value.reshape(tok_rows, GROUPS * HEAD_DIM),
+                ],
+                axis=1,
+            ),
+        )
+
+    grad_query, kv_terms = lax.scan(
+        back_step,
+        jnp.zeros((tok_rows, GROUPS, repeat, HEAD_DIM), jnp.float32),
+        (key_blocks, place_blocks, value_blocks),
+    )
+    grad_query = grad_query * score_scale
+    kv_own = lax.psum_scatter(
+        kv_terms.reshape(blocks * tok_rows, 2 * GROUPS * HEAD_DIM).astype(jnp.bfloat16),
+        "ctx",
+        scatter_dimension=0,
+        tiled=True,
+    ).astype(jnp.float32)
+    grad_key_own = kv_own[:, : GROUPS * HEAD_DIM].reshape(tok_rows, GROUPS, HEAD_DIM)
+    grad_value_own = kv_own[:, GROUPS * HEAD_DIM :].reshape(tok_rows, GROUPS, HEAD_DIM)
+    grad_qkv_f, grad_q_gain, grad_k_gain = pull_heads(
+        (grad_query.reshape(tok_rows, HEADS, HEAD_DIM), grad_key_own, grad_value_own)
+    )
+    grad_qkv_b = grad_qkv_f.astype(jnp.bfloat16)
+    grad_qkv_w = grad_half(h_attn, grad_qkv_b, w_qkv.shape[0])
+    grad_h_attn = jnp.dot(grad_qkv_b, qkv_w.T, preferred_element_type=jnp.float32)
+    grad_here_part, grad_attn_gain = pull_attn(grad_h_attn)
+    grad_inputs = (grad_residual + grad_here_part).astype(jnp.bfloat16)[None]
+    grad_qkv_own, grad_out_own, grad_gateup_own, grad_down_own = scatter_all(
+        (grad_qkv_w, grad_out_w, grad_gateup, grad_down), zfirst=(1,)
     )
     gain_attn, gain_query, gain_key, gain_ffn = lax.psum(
         (grad_attn_gain, grad_q_gain, grad_k_gain, grad_ffn_gain), ("dp", "ctx")
@@ -273,6 +899,8 @@
         P(("dp", "ctx"), None),
         P(("dp", "ctx"), None),
     )
+    fast = dict(mesh.shape) == {"dp": 4, "ctx": 8}
+    per_device = per_device_fast if fast else per_device_plain
     return jax.shard_map(
         per_device, mesh=mesh, in_specs=in_specs, out_specs=out_specs, check_vma=False
     )

time: 1140 us -> 658 us (0.58); the launches traced: 1140 us -> 647 us
  waiting for transfers between devices: 788 us -> 52 us
  Pallas kernels: 0 us -> 226 us
  local copies, waits for them, and re-layouts: 39.5 us -> 53.2 us
  other arithmetic: 45.7 us -> 58.1 us
    reduce_scatter x5 -> x1, waiting for transfers between devices: 581 us -> 20.2 us  [per_device_fast(): lax.psum_scatter(kv_terms.reshape(blocks * tok_rows, 2 * GROUPS * HEAD_DI...]
    pallas_call x0 -> x2, Pallas kernels: none -> 226 us  [the longest x1 115 us: gather_all(): pl.pallas_call(functools.partial(ag_kernel, n, W, plane_first), out_shape...]
    all_gather x6 -> x2, waiting for transfers between devices: 205 us -> 31.7 us  [the longest x1 23.7 us: per_device_fast(): lax.all_gather(key_b, 'ctx', axis=0, tiled=True)]
    dot_general x12, matrix products: 66.2 us -> 54.6 us  [the longest x4 19.1 us: grad_half(): grad = jnp.dot(left.T, both(right), preferred_element_type=jnp.float32)]
    convert_element_type x1 -> x6, other arithmetic: 1.28 us -> 12.8 us  [the longest x1 4.23 us: per_device_fast(): h_attn = h_attn_f.astype(jnp.bfloat16)]
  transfers between devices with their start and end apart: 11 -> 11, of which waited for: 9 -> 3; matrix products, arithmetic and copies ran while one was open for 15% -> 10% of each run, Pallas kernels for 0% -> 0%
where the time goes in v1:
time: 658 us; the launch traced here: 647 us
  Pallas kernels  226 us (34%)
  matrix products  190 us (29%)
  other arithmetic  58.1 us (9%)
  local copies, waits for them, and re-layouts  53.2 us (8%)
  waiting for transfers between devices  52 us (8%)
  blocking collectives  48.6 us (7%)
  between operations  15 us (2%)
    pallas_call x1, Pallas kernels, gather_all(): pl.pallas_call(functools.partial(ag_kernel, n, W, plane_first), out_shape...  115 us
    pallas_call x1, Pallas kernels, scatter_all(): pl.pallas_call(functools.partial(rs_kernel, n, W, zfirst), out_shape=outs...  110 us
    dot_general x16, matrix products, score_block(): jnp.einsum('igrd,jgd->grij', query_b, key_blk, preferred_element_type=jnp...  43.1 us
    psum x1, blocking collectives, per_device_fast(): lax.psum((grad_attn_gain, grad_q_gain, grad_k_gain, grad_ffn_gain), ('dp'...  39.7 us
    reduce_sum x8, other arithmetic, max_step(): jnp.sum(jnp.where(allowed, jnp.exp(scores - new_top[..., None]), 0.0), ax...  25.7 us
    dot_general x8, matrix products, back_step(): jnp.einsum('igrd,jgd->grij', grad_mixed_b, value_blk, preferred_element_t...  24.5 us
    dot_general x8, matrix products, out_step(): jnp.einsum('grij,jgd->igrd', weights_b, entries[2], preferred_element_typ...  23.8 us
    all_gather x1, waiting for transfers between devices, per_device_fast(): lax.all_gather(key_b, 'ctx', axis=0, tiled=True)  23.7 us
  transfers between devices with their start and end apart: 11, of which 3 were waited for; matrix products, arithmetic and copies ran while one was open for 10% of the time, Pallas kernels for 0%

profile of v1, /device:TPU:0, one launch (start us, length us, event | category | flops | bytes accessed | tf_op | source)
XLA Modules:
  0.0 647.0 jit_solution(17828194873379553341)
XLA Ops:
  8.8 115.2 %gather_weights.1 = (bf16[4,2,2,2,64,1536]{5,4,3,2,1,0:T(8,128)(2,1)}, bf16[4,2,2,2,32,2048]{5,4,3,2,1,0:T(8,128)(2,1)}, bf16[4,2,2,2,64,2048]{5,4,3,2,1,0:T(8,128)(2,1)}, bf16[4,2,2,2,32,2048]{5,4,3,2,1,0:T(8,128)(2,1)}) custom-call(bf16[64,1536]{1,0:T(8,128)(2,1)} %refs_0_.1, bf16[32,2048]{1,0:T(8,128)(2,1)} %refs_1_.1, bf16[64,2048]{1,0:T(8,128)(2,1)} %refs_2_.1, ...), custom_call_target="tpu_custom_call" | custom-call | tf_op jit(solution)/shard_map/gather_weights/pallas_call | solution.py:230
  124.0 5.0 fusion.77
  132.7 8.9 %all-gather = s32[1,2048]{1,0:T(1,128)S(1)} all-gather(s32[1,256]{1,0:T(1,128)S(1)} %copy-done.17), channel_id=2, replica_groups=mesh['dp'=4,'ctx'=8] {'ctx'}, dimensions={1}, use_global_device_ids=true | all-gather | bytes 9216 | tf_op jit(solution)/shard_map/all_gather | solution.py:726
  146.1 8.0 %all-gather.4.cloned.1.call-done = bf16[2048,4,64]{0,2,1:T(8,128)(2,1)} async-done(((bf16[256,4,64]{0,2,1:T(8,128)(2,1)}), bf16[2048,4,64]{0,2,1:T(8,128)(2,1)}) %all-gather.4.cloned.1.call-update) | async-done | bytes 1048592 | tf_op jit(solution)/shard_map/all_gather | solution.py:724
  156.4 23.7 %all-gather.6.cloned.1.call-done = bf16[2048,4,64]{0,2,1:T(8,128)(2,1)} async-done(((bf16[256,4,64]{0,2,1:T(8,128)(2,1)}), bf16[2048,4,64]{0,2,1:T(8,128)(2,1)}) %all-gather.6.cloned.1.call-update) | async-done | bytes 1048592 | tf_op jit(solution)/shard_map/all_gather | solution.py:723
  182.9 57.0 %while.37 = (s32[]{:T(128)}, f32[4,4,256]{2,1,0:T(4,128)S(1)}, f32[4,4,256]{2,1,0:T(4,128)S(1)}, s32[8,256]{1,0:T(8,128)S(1)}, s32[1,256]{1,0:T(1,128)S(1)}, /*i...) while((s32[]{:T(128)}, f32[4,4,256]{2,1,0:T(4,128)S(1)}, ...), condition=%wide.region_6.7_spmd.clone, body=%wide.region_3.6_spmd.clone.sunk | while | flops 142692352 | bytes 9457784 | solution.py:754
  183.0 3.7 fusion.143
  197.2 3.7 fusion.143
  204.4 3.7 fusion.143
  240.5 29.2 %while.38 = (s32[]{:T(128)}, f32[256,4,4,64]{0,3,2,1:T(8,128)S(1)}, bf16[8,256,4,64]{1,3,2,0:T(8,128)(2,1)}, s32[8,256]{1,0:T(8,128)S(1)}, s32[1,256]{1,0:T(1,12...) while((s32[]{:T(128)}, f32[256,4,4,64]{0,3,2,1:T(8,128)S(1)}, ...), condition=%wide.region_8.9_spmd.clone, body=%wide.region_7.8_spmd.clone.sunk | while | flops 273219584 | bytes 4083843 | solution.py:770
  276.0 6.2 fusion.94
  282.2 3.8 fusion.82
  287.2 4.6 multiply_reduce_fusion
  300.9 97.3 %while.39 = (s32[]{:T(128)}, f32[256,4,4,64]{0,3,2,1:T(8,128)}, bf16[8,256,512]{2,1,0:T(8,128)(2,1)}, bf16[8,256,4,64]{1,3,2,0:T(8,128)(2,1)}, s32[8,256]{1,0:T(...) while((s32[]{:T(128)}, f32[256,4,4,64]{0,3,2,1:T(8,128)}, ...), condition=%wide.region_13.14_spmd.clone, body=%wide.region_12.13_spmd.clone.sunk | while | flops 682819584 | bytes 59298096 | solution.py:834
  405.6 4.6 fusion.51
  417.0 4.1 convolution_convert_fusion.2
  421.1 20.2 %reduce-scatter.2.cloned.1.call-done = bf16[256,512]{1,0:T(8,128)(2,1)} async-done(((bf16[2048,512]{1,0:T(8,128)(2,1)}), bf16[256,512]{1,0:T(8,128)(2,1)}) %reduce-scatter.2.cloned.1.call-update) | async-done | bytes 262160 | tf_op jit(solution)/shard_map/reduce_scatter | solution.py:840
  447.6 5.2 fusion.52
  452.9 4.2 fusion.53
  463.5 5.9 convolution_convert_fusion
  469.4 4.2 convolution_convert_fusion.3
  473.7 39.7 %all-reduce.9 = (f32[2048]{0:T(1024)}, f32[64]{0:T(128)}, f32[64]{0:T(128)}, f32[2048]{0:T(1024)}) all-reduce(f32[2048]{0:T(1024)S(1)} %get-tuple-element.303, f32[64]{0:T(128)S(1)} %copy-done.43, f32[64]{0:T(128)S(1)} %get-tuple-element.307, f32[2048]{0:T(1024)S(1)} %copy-done.37), channel_id=1, replica_groups=mesh['dp'=4,'ctx'=8] {'dp','ctx'}, use_global_device_ids=true, to_apply=%region_19.20 | all-reduce | flops 4224 | bytes 33792 | tf_op jit(solution)/shard_map/psum | solution.py:859
  518.6 4.8 convolution_convert_fusion.1
  523.5 110.4 %scatter_grads.1 = (f32[64,1536]{1,0:T(8,128)}, f32[32,2048]{1,0:T(8,128)}, f32[64,2048]{1,0:T(8,128)}, f32[32,2048]{1,0:T(8,128)}) custom-call(bf16[4,2,2,64,1536]{4,3,2,1,0:T(8,128)(2,1)} %bitcast.309, bf16[4,2,2,32,2048]{4,3,2,1,0:T(8,128)(2,1)} %bitcast.314, bf16[4,2,2,64,2048]{4,3,2,1,0:T(8,128)(2,1)} %bitcast.307, bf16[4,2,2,32,2048]{4,3,2,1,0:T(8,128)(2,1)} %bitcast.313), custom_call_target="tpu_custom_call" | custom-call | tf_op jit(solution)/shard_map/scatter_grads/pallas_call | solution.py:439
  (434 shorter events, 240.0 us)
Async XLA Ops:
  7.2 146.9 %all-gather.4.cloned.1.call-start = ((), (), s32[]{:S(2)}) async-start(), calls=%async_computation.1 | async-start | bytes 1179648 | tf_op jit(solution)/shard_map/all_gather | solution.py:724
  8.7 115.2 %copy-start.34 = (f32[256]{0:T(256)}, f32[256]{0:T(256)S(1)}, u32[]{:S(2)}) copy-start(f32[256]{0:T(256)S(1)} %fusion.54) | copy-start | bytes 3076
  8.8 120.2 %copy-start.41 = (f32[256]{0:T(256)}, f32[256]{0:T(256)S(1)}, u32[]{:S(2)}) copy-start(f32[256]{0:T(256)S(1)} %fusion.85) | copy-start | bytes 3076
  124.0 6.2 copy-start.17
  124.0 6.5 %copy-start.38 = (f32[64]{0:T(128)S(1)}, f32[64]{0:T(128)}, u32[]{:S(2)}) copy-start(f32[64]{0:T(128)} %param.23) | copy-start | bytes 772
  129.9 50.2 %all-gather.6.cloned.1.call-start = ((), (), s32[]{:S(2)}) async-start(), calls=%async_computation.2 | async-start | bytes 1179648 | tf_op jit(solution)/shard_map/all_gather | solution.py:723
  130.2 11.9 %copy-start.25 = (f32[256,4]{0,1:T(4,128)}, f32[256,4]{0,1:T(4,128)S(1)}, u32[]{:S(2)}) copy-start(f32[256,4]{0,1:T(4,128)S(1)} %multiply_reduce_fusion.9) | copy-start | bytes 12292
  131.3 310.0 %reduce-scatter.2.cloned.1.call-start = ((), (), s32[]{:S(2)}) async-start(), calls=%async_computation.3 | async-start | bytes 2359296 | tf_op jit(solution)/shard_map/reduce_scatter | solution.py:840
  274.5 17.3 %copy-start.5 = (f32[256,2048]{1,0:T(8,128)}, f32[256,2048]{1,0:T(8,128)S(1)}, u32[]{:S(2)}) copy-start(f32[256,2048]{1,0:T(8,128)S(1)} %get-tuple-element.385) | copy-start | bytes 6291460
  274.5 17.3 %copy-start.28 = (f32[256]{0:T(256)}, f32[256]{0:T(256)S(1)}, u32[]{:S(2)}) copy-start(f32[256]{0:T(256)S(1)} %fusion.86) | copy-start | bytes 3076
  276.0 6.2 copy-start.44
  398.2 18.8 %collective-permute-start.7 = (bf16[256,2048]{1,0:T(8,128)(2,1)}, bf16[256,2048]{1,0:T(8,128)(2,1)}, u32[]{:S(2)}, u32[]{:S(2)}) collective-permute-start(bf16[256,2048]{1,0:T(8,128)(2,1)} %bitcast.14), channel_id=1, source_target_pairs={{0,1},{1,0},{2,3},{3,2},{4,5},{5,4},{6,7},{7,6},{8,9},{9,8},{10,11... | collective-permute-start | bytes 3145736 | tf_op jit(solution)/shard_map/ppermute | solution.py:702
  398.5 16.4 %collective-permute-start.2 = (bf16[256,1024]{0,1:T(8,128)(2,1)S(1)}, bf16[256,1024]{0,1:T(8,128)(2,1)}, u32[]{:S(2)}, u32[]{:S(2)}) collective-permute-start(bf16[256,1024]{0,1:T(8,128)(2,1)S(1)} %bitcast.297), channel_id=1, source_target_pairs={{0,1},{1,0},{2,3},{3,2},{4,5},{5,4},{6,7},{7,6},{8,9},{9,8},{10,11... | collective-permute-start | bytes 1572872 | tf_op jit(solution)/shard_map/ppermute | solution.py:702
  398.8 70.6 %collective-permute-start.3 = (bf16[256,2048]{1,0:T(8,128)(2,1)}, bf16[256,2048]{1,0:T(8,128)(2,1)}, u32[]{:S(2)}, u32[]{:S(2)}) collective-permute-start(bf16[256,2048]{1,0:T(8,128)(2,1)} %fusion.92), channel_id=1, source_target_pairs={{0,1},{1,0},{2,3},{3,2},{4,5},{5,4},{6,7},{7,6},{8,9},{9,8},{10,11... | collective-permute-start | bytes 3145736 | tf_op jit(solution)/shard_map/ppermute | solution.py:702
  399.0 58.1 %collective-permute-start.4 = (bf16[256,2048]{1,0:T(8,128)(2,1)}, bf16[256,2048]{1,0:T(8,128)(2,1)}, u32[]{:S(2)}, u32[]{:S(2)}) collective-permute-start(bf16[256,2048]{1,0:T(8,128)(2,1)} %multiply_convert_fusion), channel_id=1, source_target_pairs={{0,1},{1,0},{2,3},{3,2},{4,5},{5,4},{6,7},{7,6},{8,9},{9,8},{10,11... | collective-permute-start | bytes 3145736 | tf_op jit(solution)/shard_map/ppermute | solution.py:702
  399.3 11.0 %collective-permute-start.6 = (bf16[256,1024]{1,0:T(8,128)(2,1)S(1)}, bf16[256,1024]{1,0:T(8,128)(2,1)}, u32[]{:S(2)}, u32[]{:S(2)}) collective-permute-start(bf16[256,1024]{1,0:T(8,128)(2,1)S(1)} %copy-done.16), channel_id=1, source_target_pairs={{0,1},{1,0},{2,3},{3,2},{4,5},{5,4},{6,7},{7,6},{8,9},{9,8},{10,11... | collective-permute-start | bytes 1572872 | tf_op jit(solution)/shard_map/ppermute | solution.py:702
  410.3 53.2 %collective-permute-start.5 = (bf16[256,2048]{1,0:T(8,128)(2,1)}, bf16[256,2048]{1,0:T(8,128)(2,1)}, u32[]{:S(2)}, u32[]{:S(2)}) collective-permute-start(bf16[256,2048]{1,0:T(8,128)(2,1)} %add_convert_fusion), channel_id=1, source_target_pairs={{0,1},{1,0},{2,3},{3,2},{4,5},{5,4},{6,7},{7,6},{8,9},{9,8},{10,11... | collective-permute-start | bytes 3145736 | tf_op jit(solution)/shard_map/ppermute | solution.py:702
  421.1 22.1 %copy-start.39 = (f32[64]{0:T(128)S(1)}, f32[64]{0:T(128)}, u32[]{:S(2)}) copy-start(f32[64]{0:T(128)} %param.23) | copy-start | bytes 772
  421.1 22.3 %copy-start.26 = (f32[256,4]{0,1:T(4,128)S(1)}, f32[256,4]{0,1:T(4,128)}, u32[]{:S(2)}) copy-start(f32[256,4]{0,1:T(4,128)} %copy-done.25) | copy-start | bytes 12292
  447.6 5.3 copy-start.11
  457.1 56.2 %collective-permute-start = (bf16[256,2048]{1,0:T(8,128)(2,1)}, bf16[256,2048]{1,0:T(8,128)(2,1)S(1)}, u32[]{:S(2)}, u32[]{:S(2)}) collective-permute-start(bf16[256,2048]{1,0:T(8,128)(2,1)} %get-tuple-element.374), channel_id=1, source_target_pairs={{0,1},{1,0},{2,3},{3,2},{4,5},{5,4},{6,7},{7,6},{8,9},{9,8},{10,11... | collective-permute-start | bytes 3145736 | tf_op jit(solution)/shard_map/ppermute | solution.py:702
  462.9 55.7 %collective-permute-start.1 = (bf16[256,1536]{1,0:T(8,128)(2,1)}, bf16[256,1536]{1,0:T(8,128)(2,1)}, u32[]{:S(2)}, u32[]{:S(2)}) collective-permute-start(bf16[256,1536]{1,0:T(8,128)(2,1)} %add_convert_fusion.1), channel_id=1, source_target_pairs={{0,1},{1,0},{2,3},{3,2},{4,5},{5,4},{6,7},{7,6},{8,9},{9,8},{10,11... | collective-permute-start | bytes 2359304 | tf_op jit(solution)/shard_map/ppermute | solution.py:702
  463.5 5.9 copy-start.15
  633.9 5.4 copy-start.20
  (69 other events, 204.1 us)
Sparse Core Ops, SparseCore 0:
  130.1 23.9 all-gather.3
  156.5 23.5 all-gather.5
  398.3 42.9 reduce-scatter.1
